TPU v7x, 128 devices: a whole 4x4x4 slice. The times are simulated.
128 devices in a mesh: cfg: 2 (over core), seq: 32 (over y, z_lo, x), head: 2 (over z_hi).
Axes of the slice: x: 4, y: 4, z: 4 (z_hi: 2, z_lo: 2; z = z_hi * 2 + z_lo), core: 2. Of those that a mesh axis runs over, the one named last changes fastest.
Arguments:
- hidden: bfloat16 [2, 7168, 5120], P('cfg', 'seq', 'head'), may hold values from -6 to 6
- queries: bfloat16 [2, 7168, 2560], P('cfg', 'seq', 'head'), may hold values from -66 to 66
- keys: bfloat16 [2, 7168, 2560], P('cfg', 'seq', 'head'), may hold values from -12 to 12
- values: bfloat16 [2, 7168, 2560], P('cfg', 'seq', 'head'), may hold values from -6 to 6
- output_weight: bfloat16 [2560, 5120], P('head'), may hold values from -0.125 to 0.125
- adapter_down_weight: bfloat16 [8, 2560, 32], P(None, 'head'), may hold values from -0.125 to 0.125
- adapter_up_weight: bfloat16 [8, 32, 5120], P(None, None, 'head'), may hold values from -1 to 1
- request_adapters: int32 [4], replicated, may hold values from 0 to 7
- request_length: int32 [4], replicated, may hold values from 1 to 4480, 7168 in all
Outputs:
- guided: bfloat16 [7168, 5120], P('seq', 'head')
All inputs are finite; a program needn't handle non-finite values.
Results may differ from a plain program's by a relative error of at most 0.028.
Values may be sent and summed in bfloat16 or wider, within the bound.
A program may use at most 192 MiB of HBM per device.

v0:
```python
import math

import jax
import jax.numpy as jnp
from jax import lax
from jax.sharding import PartitionSpec as P

HS = 128


guide_scale = 5.0


def absorb(state, query_blocks, query_seg, key_blocks, value_blocks, key_seg):
    output_sum, row_max, row_total = state
    inverse_root = 1.0 / math.sqrt(query_blocks.shape[2])
    scores = (
        jnp.einsum("qhd,khd->hqk", query_blocks, key_blocks, preferred_element_type=jnp.float32)
        * inverse_root
    )
    same_request = (query_seg[:, None] == key_seg[None, :])[None]
    scores = jnp.where(same_request, scores, -1e30)
    new_max = jnp.maximum(row_max, jnp.max(scores, 2))
    expon = jnp.where(same_request, jnp.exp(scores - new_max[:, :, None]), 0.0)
    shrink = jnp.exp(row_max - new_max)
    row_total = row_total * shrink + jnp.sum(expon, 2)
    weighted = jnp.einsum(
        "hqk,khd->hqd", expon.astype(jnp.bfloat16), value_blocks, preferred_element_type=jnp.float32
    )
    output_sum = output_sum * shrink[:, :, None] + weighted
    return (output_sum, new_max, row_total)


def local(
    hidden,
    queries,
    keys,
    values,
    output_weight,
    adapter_down_weight,
    adapter_up_weight,
    request_adapters,
    request_length,
):
    tok_rows = queries.shape[1]
    head_width = queries.shape[2]
    local_heads = head_width // HS
    cycle_index = lax.axis_index("seq")
    request_ends = jnp.cumsum(request_length)

    def segments(start, count):
        positions = start + jnp.arange(count, dtype=jnp.int32)
        return jnp.sum((positions[:, None] >= request_ends[None, :]).astype(jnp.int32), 1)

    query_seg = segments(cycle_index * tok_rows, tok_rows)
    empty = (
        jnp.zeros((local_heads, tok_rows, HS), jnp.float32),
        jnp.full((local_heads, tok_rows), -1e30, jnp.float32),
        jnp.zeros((local_heads, tok_rows), jnp.float32),
    )
    query_blocks = queries[0].reshape(tok_rows, local_heads, HS)
    key_piece = lax.all_gather(keys[0], "seq", axis=0, tiled=True)
    value_piece = lax.all_gather(values[0], "seq", axis=0, tiled=True)
    count = key_piece.shape[0]
    blocks = count // tok_rows
    key_stack = key_piece.reshape(blocks, tok_rows, local_heads, HS)
    value_stack = value_piece.reshape(blocks, tok_rows, local_heads, HS)
    seg_stack = segments(jnp.int32(0), count).reshape(blocks, tok_rows)

    def one_block(inner_state, items):
        return (absorb(inner_state, query_blocks, query_seg, items[0], items[1], items[2]), None)

    result, unused = lax.scan(one_block, empty, (key_stack, value_stack, seg_stack))
    output_sum, row_max, row_total = result
    attention_result = (
        (output_sum / row_total[:, :, None])
        .transpose(1, 0, 2)
        .reshape(tok_rows, head_width)
        .astype(jnp.bfloat16)
    )
    projected_output = jnp.dot(attention_result, output_weight, preferred_element_type=jnp.float32)
    adapter_number = adapter_down_weight.shape[0]
    rank_columns = adapter_down_weight.shape[2]
    request_match = (
        query_seg[:, None] == jnp.arange(request_adapters.shape[0], dtype=jnp.int32)[None, :]
    )
    row_adapter = jnp.sum(jnp.where(request_match, request_adapters[None, :], 0), 1)
    picked = (row_adapter[:, None] == jnp.arange(adapter_number, dtype=jnp.int32)[None, :]).astype(
        jnp.float32
    )
    down_every_row = jnp.einsum(
        "pv,dvl->pdl", attention_result, adapter_down_weight, preferred_element_type=jnp.float32
    )
    inner_part = jnp.sum(down_every_row * picked[:, :, None], 1)
    inner_value = lax.psum(inner_part, "head").astype(jnp.bfloat16)
    expanded = (picked.astype(jnp.bfloat16)[:, :, None] * inner_value[:, None, :]).reshape(
        tok_rows, adapter_number * rank_columns
    )
    half_model_width = adapter_up_weight.shape[2]
    adapter_term = jnp.dot(
        expanded,
        adapter_up_weight.reshape(adapter_number * rank_columns, half_model_width),
        preferred_element_type=jnp.float32,
    )
    branch_factor = jnp.where(lax.axis_index("cfg") == 0, guide_scale, 1.0 - guide_scale).astype(
        jnp.float32
    )
    matching_terms = branch_factor * (hidden[0].astype(jnp.float32) + adapter_term)
    half = lax.psum_scatter(
        (branch_factor * projected_output).astype(jnp.bfloat16),
        "head",
        scatter_dimension=1,
        tiled=True,
    ).astype(jnp.float32)
    guided = lax.psum((half + matching_terms).astype(jnp.bfloat16), "cfg")
    return guided


def solution(mesh):
    return jax.shard_map(
        local,
        mesh=mesh,
        in_specs=(
            P("cfg", "seq", "head"),
            P("cfg", "seq", "head"),
            P("cfg", "seq", "head"),
            P("cfg", "seq", "head"),
            P("head", None),
            P(None, "head", None),
            P(None, None, "head"),
            P(),
            P(),
        ),
        out_specs=P("seq", "head"),
        check_vma=False,
    )
```

profile of v0, /device:TPU:1, one launch (start us, length us, event | category | flops | bytes accessed | tf_op | source)
XLA Modules:
  0.0 854.1 jit_solution(5007075119378924658)
XLA Ops:
  10.9 208.3 %all-gather.5.cloned.1.call-done = bf16[1,7168,1280]{2,1,0:T(8,128)(2,1)} async-done(((bf16[1,224,1280]{2,1,0:T(8,128)(2,1)}), bf16[1,7168,1280]{2,1,0:T(8,128)(2,1)}) %all-gather.5.cloned.1.call-update) | async-done | bytes 18350096 | tf_op jit(solution)/shard_map/all_gather | solution.py:62
  219.2 35.9 %reshape.130 = bf16[32,224,10,128]{3,2,1,0:T(8,128)(2,1)} reshape(bf16[1,7168,1280]{2,1,0:T(8,128)(2,1)} %all-gather.5.cloned.1.call-done) | data formatting | bytes 36700160 | tf_op jit(solution)/shard_map/reshape | solution.py:66
  255.1 19.7 %copy.25 = bf16[32,224,10,128]{3,1,2,0:T(8,128)(2,1)} copy(bf16[32,224,10,128]{3,2,1,0:T(8,128)(2,1)} %reshape.130) | data formatting | bytes 36700160
  274.7 150.7 %all-gather.7.cloned.1.call-done = bf16[1,7168,1280]{2,1,0:T(8,128)(2,1)} async-done(((bf16[1,224,1280]{2,1,0:T(8,128)(2,1)}), bf16[1,7168,1280]{2,1,0:T(8,128)(2,1)}) %all-gather.7.cloned.1.call-update) | async-done | bytes 18350096 | tf_op jit(solution)/shard_map/all_gather | solution.py:63
  425.4 35.8 %reshape.131 = bf16[32,224,10,128]{3,2,1,0:T(8,128)(2,1)} reshape(bf16[1,7168,1280]{2,1,0:T(8,128)(2,1)} %all-gather.7.cloned.1.call-done) | data formatting | bytes 36700160 | tf_op jit(solution)/shard_map/reshape | solution.py:67
  461.3 19.4 %copy.27 = bf16[32,224,10,128]{3,1,2,0:T(8,128)(2,1)} copy(bf16[32,224,10,128]{3,2,1,0:T(8,128)(2,1)} %reshape.131) | data formatting | bytes 36700160
  480.7 289.0 %while.15 = (s32[]{:T(128)}, f32[10,224,128]{2,1,0:T(8,128)}, f32[10,224]{1,0:T(8,128)S(1)}, f32[10,224]{1,0:T(8,128)S(1)}, s32[224]{0:T(256)S(1)}, /*index=5*/s...) while((s32[]{:T(128)}, f32[10,224,128]{2,1,0:T(8,128)}, ...), condition=%wide.region_6.7_spmd.clone, body=%wide.region_3.6_spmd.clone.sunk | while | flops 264345536 | bytes 18412184 | solution.py:73
  480.8 3.0 fusion.47
  486.3 3.1 convolution_add_fusion.2
  489.5 3.0 fusion.47
  494.9 3.5 convolution_add_fusion.2
  504.0 3.5 convolution_add_fusion.2
  507.6 3.0 fusion.47
  513.0 3.5 convolution_add_fusion.2
  516.6 3.0 fusion.47
  522.1 3.5 convolution_add_fusion.2
  531.1 3.5 convolution_add_fusion.2
  534.7 3.0 fusion.47
  540.2 3.5 convolution_add_fusion.2
  543.8 3.0 fusion.47
  549.2 3.5 convolution_add_fusion.2
  558.2 3.5 convolution_add_fusion.2
  561.8 3.0 fusion.47
  567.3 3.5 convolution_add_fusion.2
  570.9 3.0 fusion.47
  576.3 3.5 convolution_add_fusion.2
  585.4 3.5 convolution_add_fusion.2
  589.0 3.0 fusion.47
  594.4 3.5 convolution_add_fusion.2
  598.0 3.0 fusion.47
  603.5 3.5 convolution_add_fusion.2
  612.5 3.5 convolution_add_fusion.2
  616.1 3.0 fusion.47
  621.6 3.5 convolution_add_fusion.2
  625.2 3.0 fusion.47
  630.6 3.5 convolution_add_fusion.2
  639.6 3.5 convolution_add_fusion.2
  643.2 3.0 fusion.47
  648.7 3.5 convolution_add_fusion.2
  652.3 3.0 fusion.47
  657.7 3.5 convolution_add_fusion.2
  666.8 3.5 convolution_add_fusion.2
  670.4 3.0 fusion.47
  675.8 3.5 convolution_add_fusion.2
  679.4 3.0 fusion.47
  684.9 3.5 convolution_add_fusion.2
  693.9 3.5 convolution_add_fusion.2
  697.5 3.0 fusion.47
  703.0 3.5 convolution_add_fusion.2
  706.6 3.0 fusion.47
  712.0 3.5 convolution_add_fusion.2
  721.0 3.5 convolution_add_fusion.2
  730.1 3.5 convolution_add_fusion.2
  733.7 3.0 fusion.47
  739.1 3.5 convolution_add_fusion.2
  748.2 3.5 convolution_add_fusion.2
  757.2 3.5 convolution_add_fusion.2
  760.8 3.0 fusion.47
  766.3 3.5 convolution_add_fusion.2
  771.6 9.3 %fusion.20 = bf16[224,5120]{1,0:T(8,128)(2,1)} fusion(bf16[224,1280]{0,1:T(8,128)(2,1)S(1)} %bitcast.63, bf16[1280,5120]{1,0:T(8,128)(2,1)} %param.15, f32[]{:T(128)S(6)} %select_n.15), kind=kOutput, calls=%fused_computation.29 | convolution fusion | flops 2938306560 | bytes 15974404 | tf_op jit(solution)/shard_map/dot_general | solution.py:81
  782.4 9.6 %psum.14 = bf16[224,32]{0,1:T(8,128)(2,1)S(1)} all-reduce(f32[224,32]{0,1:T(8,128)S(1)} %multiply_reduce_fusion), channel_id=1, replica_groups=mesh['cfg'=2,'seq'=32,'head'=2] {'head'}, use_global_device_ids=true, to_apply=%region_10.11 | all-reduce | flops 7168 | bytes 43008 | tf_op jit(solution)/shard_map/psum | solution.py:95
  792.1 25.2 %reduce-scatter.2.cloned.1.call-done = bf16[224,2560]{1,0:T(8,128)(2,1)} async-done(((bf16[224,5120]{1,0:T(8,128)(2,1)}), bf16[224,2560]{1,0:T(8,128)(2,1)}) %reduce-scatter.2.cloned.1.call-update) | async-done | bytes 1146896 | tf_op jit(solution)/shard_map/reduce_scatter | solution.py:109
  817.3 3.2 fusion.24
  820.5 24.8 %all-reduce.2.cloned.1.call-done = bf16[224,2560]{1,0:T(8,128)(2,1)} async-done(((bf16[224,2560]{1,0:T(8,128)(2,1)}), bf16[224,2560]{1,0:T(8,128)(2,1)}) %all-reduce.2.cloned.1.call-update) | async-done | bytes 1146896 | tf_op jit(solution)/shard_map/psum | solution.py:115
  (299 shorter events, 126.9 us)
Async XLA Ops:
  6.5 810.7 %copy-start = (bf16[8,32,2560]{2,1,0:T(8,128)(2,1)S(1)}, bf16[8,32,2560]{2,1,0:T(8,128)(2,1)}, u32[]{:S(2)}) copy-start(bf16[8,32,2560]{2,1,0:T(8,128)(2,1)} %param.17) | copy-start | bytes 3932164
  6.5 212.7 %all-gather.5.cloned.1.call-start = ((), (), s32[]{:S(2)}) async-start(), calls=%async_computation.3 | async-start | bytes 18923520 | tf_op jit(solution)/shard_map/all_gather | solution.py:62
  7.3 418.2 %all-gather.7.cloned.1.call-start = ((), (), s32[]{:S(2)}) async-start(), calls=%async_computation.4 | async-start | bytes 18923520 | tf_op jit(solution)/shard_map/all_gather | solution.py:63
  8.0 809.3 %reduce-scatter.2.cloned.1.call-start = ((), (), s32[]{:S(2)}) async-start(), calls=%async_computation.1 | async-start | bytes 3440640 | tf_op jit(solution)/shard_map/reduce_scatter | solution.py:109
  483.8 2.4 copy-start.1
  492.5 2.4 copy-start.1
  501.5 2.4 copy-start.1
  510.6 2.4 copy-start.1
  519.6 2.4 copy-start.1
  528.7 2.4 copy-start.1
  537.7 2.4 copy-start.1
  546.8 2.4 copy-start.1
  555.8 2.4 copy-start.1
  564.8 2.4 copy-start.1
  573.9 2.4 copy-start.1
  582.9 2.4 copy-start.1
  592.0 2.4 copy-start.1
  601.0 2.4 copy-start.1
  610.1 2.4 copy-start.1
  619.1 2.4 copy-start.1
  628.2 2.4 copy-start.1
  637.2 2.4 copy-start.1
  646.2 2.4 copy-start.1
  655.3 2.4 copy-start.1
  664.3 2.4 copy-start.1
  673.4 2.4 copy-start.1
  682.4 2.4 copy-start.1
  691.5 2.4 copy-start.1
  700.5 2.4 copy-start.1
  709.6 2.4 copy-start.1
  718.6 2.4 copy-start.1
  727.6 2.4 copy-start.1
  736.7 2.4 copy-start.1
  745.7 2.4 copy-start.1
  754.8 2.4 copy-start.1
  763.8 2.4 copy-start.1
  780.9 0.7 copy-start.3
  780.9 1.1 copy-start.2
  781.0 64.3 %all-reduce.2.cloned.1.call-start = ((), (), s32[]{:S(2)}) async-start(), calls=%async_computation.2 | async-start | bytes 2293760 | tf_op jit(solution)/shard_map/psum | solution.py:115
Sparse Core Ops, SparseCore 0:
  9.0 210.1 all-gather.4
  220.8 204.5 all-gather.6
  781.1 36.1 reduce-scatter.1
  820.6 24.5 all-reduce.1
where the time goes:
time: 859 us; the launch traced here: 854 us
  waiting for transfers between devices  410 us (48%)
  matrix products  220 us (26%)
  local copies, waits for them, and re-layouts  116 us (14%)
  other arithmetic  83.5 us (10%)
  between operations  13.2 us (2%)
  blocking collectives  9.62 us (1%)
    all_gather x1, waiting for transfers between devices, local(): key_piece = lax.all_gather(keys[0], 'seq', axis=0, tiled=True)  208 us
    all_gather x1, waiting for transfers between devices, local(): value_piece = lax.all_gather(values[0], 'seq', axis=0, tiled=True)  151 us
    dot_general x32, matrix products, absorb(): jnp.einsum('hqk,khd->hqd', expon.astype(jnp.bfloat16), value_blocks, pref...  111 us
    dot_general x32, matrix products, absorb(): jnp.einsum('qhd,khd->hqk', query_blocks, key_blocks, preferred_element_ty...  95.9 us
    reduce_sum x32, other arithmetic, absorb(): row_total = row_total * shrink + jnp.sum(expon, 2)  76.8 us
    unnamed x11, local copies, waits for them, and re-layouts  44 us
    reshape x1, local copies, waits for them, and re-layouts, local(): key_stack = key_piece.reshape(blocks, tok_rows, local_heads, HS)  35.9 us
    reshape x1, local copies, waits for them, and re-layouts, local(): value_stack = value_piece.reshape(blocks, tok_rows, local_heads, HS)  35.8 us
  transfers between devices with their start and end apart: 4, of which 4 were waited for; matrix products, arithmetic and copies ran while one was open for 7% of the time, Pallas kernels for 0%

commit v1 on v0

v1 whole, which is shorter than its diff:
```python
import functools
import math

import jax
import jax.numpy as jnp
from jax import lax
from jax.experimental import pallas as pl
from jax.experimental.pallas import tpu as pltpu
from jax.sharding import PartitionSpec as P

MESH = pl.DeviceIdType.MESH
HS = 128
GUIDE = 5.0
BK = 512
ANY = pl.BlockSpec(memory_space=pl.ANY)
SMEM = pl.BlockSpec(memory_space=pltpu.SMEM)


def place(head, branch):
    p = (head // 2) * 3 + head % 2
    return (p // 4) * 8 + branch * 4 + p % 4


def role(s):
    p = (s // 8) * 4 + s % 4
    active = jnp.logical_and(p % 3 < 2, p < 15)
    head = (p // 3) * 2 + p % 3
    return active, head, (s // 4) % 2


def scatter_kernel(
    q_ref, k_ref, v_ref, hid_ref, kbuf, vbuf, qbuf, hbuf,
    send_sem, kv_sem, q_sem, hid_sem, fwd_sem,
):
    b = lax.axis_index("cfg")
    s = lax.axis_index("seq")
    g = lax.axis_index("head")
    rows = q_ref.shape[1]
    heads = q_ref.shape[2] // HS
    half = hbuf.shape[1]
    groups = kv_sem.shape[0]
    per = kbuf.shape[0] // groups

    other = pltpu.make_async_remote_copy(
        src_ref=hid_ref.at[0, :, pl.ds(pl.multiple_of((1 - b) * half, half), half)],
        dst_ref=hbuf,
        send_sem=hid_sem.at[0],
        recv_sem=hid_sem.at[1],
        device_id=(1 - b, s, g),
        device_id_type=MESH,
    )

    row0 = pl.multiple_of(s * rows, 32)
    qrow0 = pl.multiple_of((s // 2) * rows, 32)
    kind = (
        (k_ref, lambda: kbuf.at[pl.ds(row0, rows), :], kv_sem.at[s // (32 // groups)], 0),
        (v_ref, lambda: vbuf.at[pl.ds(row0, rows), :], kv_sem.at[s // (32 // groups)], 1),
        (q_ref, lambda: qbuf.at[pl.ds(qrow0, rows), :], q_sem, s % 2),
    )

    def each(i, act):
        h = (i + s) % heads
        target = place(h, b)
        for n, (src, dst, sem, core) in enumerate(kind):
            piece = src.at[0, :, pl.ds(pl.multiple_of(h * HS, HS), HS)]
            mine = jnp.logical_and(target == s, core == b)
            act(n, piece, dst(), sem, core, target, mine, i)

    def start(n, piece, dst, sem, core, target, mine, i):
        @pl.when(mine)
        def _():
            pltpu.make_async_copy(piece, dst, sem).start()

        @pl.when(jnp.logical_not(mine))
        def _():
            pltpu.make_async_remote_copy(
                src_ref=piece, dst_ref=dst, send_sem=send_sem.at[i * 3 + n], recv_sem=sem,
                device_id=(core, target, g), device_id_type=MESH,
            ).start()

    def finish(n, piece, dst, sem, core, target, mine, i):
        @pl.when(jnp.logical_not(mine))
        def _():
            pltpu.make_async_remote_copy(
                src_ref=piece, dst_ref=dst, send_sem=send_sem.at[i * 3 + n], recv_sem=sem,
                device_id=(core, target, g), device_id_type=MESH,
            ).wait_send()

    @pl.loop(0, heads)
    def _(i):
        each(i, start)

    other.start()

    active, _, _ = role(s)

    def forward(buf, n):
        part = buf.at[pl.ds(n * per, per), :]
        return pltpu.make_async_remote_copy(
            src_ref=part, dst_ref=part, send_sem=fwd_sem.at[0, n], recv_sem=fwd_sem.at[1, n],
            device_id=(1 - b, s, g), device_id_type=MESH,
        )

    def landed(buf, sem):
        pltpu.make_async_copy(buf, buf, sem).wait()

    for core, (got, came) in enumerate(((kbuf, vbuf), (vbuf, kbuf))):

        @pl.when(jnp.logical_and(active, b == core))
        def _():
            for n in range(groups):
                landed(got.at[pl.ds(n * per, per), :], kv_sem.at[n])
                forward(got, n).start()
            for n in range(groups):
                forward(got, n).wait_send()
                forward(came, n).wait_recv()
            landed(qbuf, q_sem)

    @pl.loop(0, heads)
    def _(i):
        each(i, finish)

    other.wait()


def attention_kernel(len_ref, q_ref, k_ref, v_ref, o_ref, s_ref, m_ref, l_ref, acc_ref):
    c = lax.axis_index("cfg")
    s = lax.axis_index("seq")
    active, _, _ = role(s)
    rows = q_ref.shape[0]
    tokens = k_ref.shape[0]
    factor = math.log2(math.e) / math.sqrt(HS)
    first = (2 * pl.program_id(0) + c) * rows
    last = first + rows - 1
    e0 = len_ref[0]
    e1 = e0 + len_ref[1]
    e2 = e1 + len_ref[2]

    def segment(pos):
        return (
            (pos >= e0).astype(jnp.int32)
            + (pos >= e1).astype(jnp.int32)
            + (pos >= e2).astype(jnp.int32)
        )

    @pl.when(active)
    def _():
        seg_first = segment(first)
        seg_last = segment(last)
        starts = (0, e0, e1, e2)
        ends = (e0, e1, e2, tokens)
        lo = jnp.int32(0)
        hi = jnp.int32(tokens)
        for n in range(4):
            lo = jnp.where(seg_first == n, starts[n], lo)
            hi = jnp.where(seg_last == n, ends[n], hi)
        base = (lo // 32) * 32
        blocks = pl.cdiv(hi - base, BK)
        single = seg_first == seg_last
        seg_q = segment(first + lax.broadcasted_iota(jnp.int32, (rows, 1), 0))
        q = q_ref[...]
        m_ref[...] = jnp.full_like(m_ref, -1e30)

        def lanes(x, op):
            out = x[:, :HS]
            for n in range(1, BK // HS):
                out = op(out, x[:, n * HS : (n + 1) * HS])
            return out

        @pl.loop(0, blocks)
        def _(n):
            logical = base + n * BK
            at = pl.multiple_of(jnp.minimum(logical, tokens - BK), 32)
            score = lax.dot_general(
                q, k_ref[pl.ds(at, BK), :], (((1,), (1,)), ((), ())),
                preferred_element_type=jnp.float32,
            )
            whole = jnp.logical_and(
                single, jnp.logical_and(logical >= lo, logical + BK <= hi)
            )

            @pl.when(whole)
            def _():
                s_ref[n] = score
                m_ref[...] = jnp.maximum(m_ref[...], lanes(score, jnp.maximum))

            @pl.when(jnp.logical_not(whole))
            def _():
                pos = at + lax.broadcasted_iota(jnp.int32, (1, BK), 1)
                seg_k = jnp.where(pos >= logical, segment(pos), -1)
                masked = jnp.where(seg_q == seg_k, score, -jnp.inf)
                s_ref[n] = masked
                m_ref[...] = jnp.maximum(m_ref[...], lanes(masked, jnp.maximum))

        top = jnp.max(m_ref[...], axis=1, keepdims=True)
        l_ref[...] = jnp.zeros_like(l_ref)
        acc_ref[...] = jnp.zeros_like(acc_ref)

        @pl.loop(0, blocks)
        def _(n):
            at = pl.multiple_of(jnp.minimum(base + n * BK, tokens - BK), 32)
            weight = jnp.exp2((s_ref[n] - top) * factor)
            l_ref[...] += lanes(weight, jnp.add)
            acc_ref[...] += jnp.dot(
                weight.astype(jnp.bfloat16), v_ref[pl.ds(at, BK), :],
                preferred_element_type=jnp.float32,
            )

        total = jnp.sum(l_ref[...], axis=1, keepdims=True)
        o_ref[...] = (acc_ref[...] / total).astype(o_ref.dtype)


def project_kernel(
    len_ref, ad_ref, o_ref, hid_ref, hbuf, w_ref, down_ref, up_ref, out_ref,
    att, wo, wm, downv, upv, hm, ho, dv, pm, psend, precv, isend, irecv, outv,
    load_sem, o_send, o_sem, att_sem, p_sem, i_sem, out_sem,
):
    b = lax.axis_index("cfg")
    s = lax.axis_index("seq")
    g = lax.axis_index("head")
    active, head, branch = role(s)
    rows, half = outv.shape
    width = 2 * half
    blocks = o_ref.shape[0] // rows
    mine = pl.multiple_of(b * half, half)

    loads = [
        (down_ref, downv),
        (w_ref.at[:, pl.ds(pl.multiple_of((1 - g) * width + b * half, half), half)], wo),
        (w_ref.at[:, pl.ds(pl.multiple_of(g * width + b * half, half), half)], wm),
        (up_ref.at[:, pl.ds(mine, half)], upv),
        (hid_ref.at[0, :, pl.ds(mine, half)], hm),
        (hbuf, ho),
    ]
    loads = [pltpu.make_async_copy(a, z, load_sem.at[n]) for n, (a, z) in enumerate(loads)]

    def send_o(i, go):
        j = 2 * i + b
        piece = o_ref.at[pl.ds(pl.multiple_of(i * rows, 32), rows), :]
        dst = att.at[branch, :, pl.ds(pl.multiple_of(head * HS, HS), HS)]
        here = jnp.logical_and(j == s, branch == b)

        @pl.when(here)
        def _():
            if go:
                pltpu.make_async_copy(piece, dst, o_sem).start()

        @pl.when(jnp.logical_not(here))
        def _():
            copy = pltpu.make_async_remote_copy(
                src_ref=piece, dst_ref=dst, send_sem=o_send.at[i], recv_sem=o_sem,
                device_id=(branch, j, g), device_id_type=MESH,
            )
            if go:
                copy.start()
            else:
                copy.wait_send()

    @pl.when(active)
    def _():
        @pl.loop(0, blocks)
        def _(i):
            send_o((i + s // 2) % blocks, True)

    for copy in loads:
        copy.start()

    pltpu.make_async_copy(att.at[b], att.at[b], o_sem).wait()
    swap = pltpu.make_async_remote_copy(
        src_ref=att.at[b], dst_ref=att.at[b], send_sem=att_sem.at[0], recv_sem=att_sem.at[1],
        device_id=(1 - b, s, g), device_id_type=MESH,
    )
    swap.start()
    swap.wait()
    dv[...] = (
        GUIDE * att[0].astype(jnp.float32) + (1.0 - GUIDE) * att[1].astype(jnp.float32)
    ).astype(jnp.bfloat16)

    def partner(src, dst, sems):
        return pltpu.make_async_remote_copy(
            src_ref=src, dst_ref=dst, send_sem=sems.at[0], recv_sem=sems.at[1],
            device_id=(b, s, 1 - g), device_id_type=MESH,
        )

    loads[0].wait()
    pos = s * rows + lax.broadcasted_iota(jnp.int32, (rows, 1), 0)
    e0 = len_ref[0]
    e1 = e0 + len_ref[1]
    e2 = e1 + len_ref[2]
    adapter = jnp.where(
        pos < e1,
        jnp.where(pos < e0, ad_ref[0], ad_ref[1]),
        jnp.where(pos < e2, ad_ref[2], ad_ref[3]),
    )
    rank = downv.shape[1] // 8
    lane = lax.broadcasted_iota(jnp.int32, (rows, downv.shape[1]), 1)
    picked = (lane // rank) == adapter
    inner = jnp.dot(dv[...], downv[...], preferred_element_type=jnp.float32)
    isend[...] = jnp.where(picked, inner, 0.0).astype(jnp.bfloat16)
    inner_copy = partner(isend, irecv, i_sem)
    inner_copy.start()

    cols = 256
    loads[1].wait()
    for n in range(half // cols):
        sl = pl.ds(n * cols, cols)
        psend[n] = jnp.dot(dv[...], wo[:, sl], preferred_element_type=jnp.float32).astype(jnp.bfloat16)
        partner(psend.at[n], precv.at[n], p_sem.at[n]).start()
    loads[2].wait()
    for n in range(half // cols):
        sl = pl.ds(n * cols, cols)
        pm[:, sl] = jnp.dot(dv[...], wm[:, sl], preferred_element_type=jnp.float32)
    for copy in loads[3:]:
        copy.wait()
    scale_m = jnp.where(b == 0, GUIDE, 1.0 - GUIDE).astype(jnp.float32)
    scale_o = jnp.where(b == 0, 1.0 - GUIDE, GUIDE).astype(jnp.float32)
    inner_copy.wait()
    both = jnp.where(
        picked, inner + irecv[...].astype(jnp.float32), 0.0
    ).astype(jnp.bfloat16)
    for n in range(half // cols):
        sl = pl.ds(n * cols, cols)
        pm[:, sl] += (
            jnp.dot(both, upv[:, sl], preferred_element_type=jnp.float32)
            + scale_m * hm[:, sl].astype(jnp.float32)
            + scale_o * ho[:, sl].astype(jnp.float32)
        )
    for n in range(half // cols):
        sl = pl.ds(n * cols, cols)
        partner(psend.at[n], precv.at[n], p_sem.at[n]).wait()
        outv[:, sl] = (pm[:, sl] + precv[n].astype(jnp.float32)).astype(jnp.bfloat16)
    result = out_ref.at[:, pl.ds(mine, half)]
    give = pltpu.make_async_remote_copy(
        src_ref=outv, dst_ref=result, send_sem=out_sem.at[0], recv_sem=out_sem.at[1],
        device_id=(1 - b, s, g), device_id_type=MESH,
    )
    keep = pltpu.make_async_copy(outv, result, out_sem.at[2])
    give.start()
    keep.start()

    @pl.when(active)
    def _():
        @pl.loop(0, blocks)
        def _(i):
            send_o(i, False)

    give.wait()
    keep.wait()


def local(
    hidden, queries, keys, values, output_weight, adapter_down_weight, adapter_up_weight,
    request_adapters, request_length,
):
    rows, width = queries.shape[1:]
    tokens = rows * 32
    bf16, f32 = jnp.bfloat16, jnp.float32
    dma = pltpu.SemaphoreType.DMA
    down = adapter_down_weight.transpose(1, 0, 2).reshape(width, -1)
    up = adapter_up_weight.reshape(-1, adapter_up_weight.shape[2])
    rank = down.shape[1]

    kbuf, vbuf, qbuf, hbuf = pl.pallas_call(
        scatter_kernel,
        out_shape=(
            jax.ShapeDtypeStruct((tokens, HS), bf16),
            jax.ShapeDtypeStruct((tokens, HS), bf16),
            jax.ShapeDtypeStruct((tokens // 2, HS), bf16),
            jax.ShapeDtypeStruct((rows, width), bf16),
        ),
        in_specs=[ANY] * 4,
        out_specs=(ANY,) * 4,
        scratch_shapes=[dma((30,)), dma((4,)), dma, dma((2,)), dma((2, 4))],
        compiler_params=pltpu.CompilerParams(has_side_effects=True),
        name="scatter_heads",
    )(queries, keys, values, hidden)

    steps = tokens // 2 // rows
    o = pl.pallas_call(
        attention_kernel,
        grid=(steps,),
        out_shape=jax.ShapeDtypeStruct((tokens // 2, HS), bf16),
        in_specs=[
            SMEM,
            pl.BlockSpec((rows, HS), lambda i: (i, 0)),
            pl.BlockSpec((tokens, HS), lambda i: (0, 0)),
            pl.BlockSpec((tokens, HS), lambda i: (0, 0)),
        ],
        out_specs=pl.BlockSpec((rows, HS), lambda i: (i, 0)),
        scratch_shapes=[
            pltpu.VMEM((tokens // BK + 1, rows, BK), f32),
            pltpu.VMEM((rows, HS), f32),
            pltpu.VMEM((rows, HS), f32),
            pltpu.VMEM((rows, HS), f32),
        ],
        compiler_params=pltpu.CompilerParams(vmem_limit_bytes=48 * 2**20),
        name="attend",
    )(request_length, qbuf, kbuf, vbuf)

    half = width
    cols = 256
    return pl.pallas_call(
        project_kernel,
        out_shape=jax.ShapeDtypeStruct((rows, 2 * half), bf16),
        in_specs=[SMEM, SMEM] + [ANY] * 6,
        out_specs=ANY,
        scratch_shapes=[
            pltpu.VMEM((2, rows, width), bf16),
            pltpu.VMEM((width, half), bf16),
            pltpu.VMEM((width, half), bf16),
            pltpu.VMEM((width, rank), bf16),
            pltpu.VMEM((rank, half), bf16),
            pltpu.VMEM((rows, half), bf16),
            pltpu.VMEM((rows, half), bf16),
            pltpu.VMEM((rows, width), bf16),
            pltpu.VMEM((rows, half), f32),
            pltpu.VMEM((half // cols, rows, cols), bf16),
            pltpu.VMEM((half // cols, rows, cols), bf16),
            pltpu.VMEM((rows, rank), bf16),
            pltpu.VMEM((rows, rank), bf16),
            pltpu.VMEM((rows, half), bf16),
            dma((6,)), dma((steps,)), dma, dma((2,)), dma((half // cols, 2)), dma((2,)), dma((3,)),
        ],
        compiler_params=pltpu.CompilerParams(
            has_side_effects=True, vmem_limit_bytes=48 * 2**20
        ),
        name="project",
    )(request_length, request_adapters, o, hidden, hbuf, output_weight, down, up)


def solution(mesh):
    return jax.shard_map(
        local,
        mesh=mesh,
        in_specs=(
            P("cfg", "seq", "head"),
            P("cfg", "seq", "head"),
            P("cfg", "seq", "head"),
            P("cfg", "seq", "head"),
            P("head", None),
            P(None, "head", None),
            P(None, None, "head"),
            P(),
            P(),
        ),
        out_specs=P("seq", "head"),
        check_vma=False,
    )
```

time: 859 us -> 180 us (0.21)
  waiting for transfers between devices: 410 us -> 0 us
  matrix products: 220 us -> 0 us
  Pallas kernels: 0 us -> 171 us
  local copies, waits for them, and re-layouts: 116 us -> 7.92 us
  other arithmetic: 83.5 us -> 0 us
  between operations: 13.2 us -> 0.09 us
  blocking collectives: 9.62 us -> 0 us
    all_gather x2 -> x0, waiting for transfers between devices: 359 us -> none  [the longest x1 208 us: local(): key_piece = lax.all_gather(keys[0], 'seq', axis=0, tiled=True)]
    dot_general x66 -> x0, matrix products: 219 us -> none  [the longest x32 111 us: absorb(): jnp.einsum('hqk,khd->hqd', expon.astype(jnp.bfloat16), value_blocks, pref...]
    pallas_call x0 -> x3, Pallas kernels: none -> 171 us  [the longest x1 60.1 us: local(): pl.pallas_call(attention_kernel, grid=(steps,), out_shape=jax.ShapeDtypeS...]
    reduce_sum x36 -> x0, other arithmetic: 77.2 us -> none  [the longest x32 76.8 us: absorb(): row_total = row_total * shrink + jnp.sum(expon, 2)]
    reshape x3 -> x1, local copies, waits for them, and re-layouts: 71.8 us -> 1.42 us  [local(): down = adapter_down_weight.transpose(1, 0, 2).reshape(width, -1)]
    unnamed x11 -> x17, local copies, waits for them, and re-layouts: 44 us -> 6.51 us
    reduce_scatter x1 -> x0, waiting for transfers between devices: 25.2 us -> none  [local(): lax.psum_scatter((branch_factor * projected_output).astype(jnp.bfloat16),...]
    psum x1 -> x0, waiting for transfers between devices: 24.8 us -> none  [local(): guided = lax.psum((half + matching_terms).astype(jnp.bfloat16), 'cfg')]
  transfers between devices with their start and end apart: 4 -> 0, of which waited for: 4 -> 0; matrix products, arithmetic and copies ran while one was open for 7% -> 0% of each run, Pallas kernels for 0% -> 0%
where the time goes in v1:
time: 180 us; the launch traced here: 179 us
  Pallas kernels  171 us (95%)
  local copies, waits for them, and re-layouts  7.92 us (4%)
    pallas_call x1, Pallas kernels, local(): pl.pallas_call(attention_kernel, grid=(steps,), out_shape=jax.ShapeDtypeS...  60.1 us
    pallas_call x1, Pallas kernels, local(): pl.pallas_call(scatter_kernel, out_shape=(jax.ShapeDtypeStruct((tokens, H...  56.7 us
    pallas_call x1, Pallas kernels, local(): pl.pallas_call(project_kernel, out_shape=jax.ShapeDtypeStruct((rows, 2 *...  54.6 us
    unnamed x17, local copies, waits for them, and re-layouts  6.51 us

profile of v1, /device:TPU:1, one launch (start us, length us, event | category | flops | bytes accessed | tf_op | source)
XLA Modules:
  0.0 179.4 jit_solution(3942499698610487454)
XLA Ops:
  0.0 0.0 copy-start.6
  0.0 56.7 %scatter_heads.1 = (bf16[7168,128]{1,0:T(8,128)(2,1)}, bf16[7168,128]{1,0:T(8,128)(2,1)}, bf16[3584,128]{1,0:T(8,128)(2,1)}, bf16[224,1280]{1,0:T(8,128)(2,1)}) custom-call(bf16[1,224,1280]{2,1,0:T(8,128)(2,1)} %q_ref.1, bf16[1,224,1280]{2,1,0:T(8,128)(2,1)} %k_ref.1, bf16[1,224,1280]{2,1,0:T(8,128)(2,1)} %v_ref.1, bf16[1,224,2560]{2,1,0:T(8,128)(2,1)} %hid_ref.3), custom_call_target="tpu_custom_call" | custom-call | tf_op jit(solution)/shard_map/scatter_heads/pallas_call | solution.py:363
  56.7 0.0 copy-done.6
  56.7 0.0 copy-start.1
  56.7 1.5 copy-done.1
  58.2 0.0 copy-start.2
  58.2 1.5 copy-done.2
  59.7 0.0 copy-start.4
  59.7 1.2 copy-done.4
  60.9 0.0 copy-start.5
  60.9 60.1 %attend.1.o_ref = bf16[3584,128]{1,0:T(8,128)(2,1)S(1)} custom-call(s32[4]{0:T(128)S(1)} %copy-done.6, bf16[3584,128]{1,0:T(8,128)(2,1)S(1)} %copy-done.4, bf16[7168,128]{1,0:T(8,128)(2,1)S(1)} %copy-done.1, bf16[7168,128]{1,0:T(8,128)(2,1)S(1)} %copy-done.2), custom_call_target="tpu_custom_call" | custom-call | tf_op jit(solution)/shard_map/attend/pallas_call | solution.py:379
  121.0 0.0 copy-start
  121.0 0.0 copy-start.7
  121.0 1.4 copy.11.down_ref
  122.4 0.0 copy-done.5
  122.4 0.0 copy-done
  122.4 0.0 copy-done.7
  122.4 0.0 copy-start.3
  122.4 1.3 copy-done.3
  123.8 54.6 %project.1 = bf16[224,2560]{1,0:T(8,128)(2,1)S(1)} custom-call(s32[4]{0:T(128)S(1)} %copy-done.6, s32[4]{0:T(128)S(1)} %copy-done.7, bf16[3584,128]{1,0:T(8,128)(2,1)S(1)} %attend.1.o_ref, bf16[1,224,2560]{2,1,0:T(8,128)(2,1)S(1)} %copy-done, bf16[224,1280]{1,0:T(8,128)(2,1)S(1)} %copy-done.5, bf16[1280,5120]{1,0:T(8,128)(2,1)} %w_ref.1, ...), custom_call_target="tpu_custom_call" | custom-call | tf_op jit(solution)/shard_map/project/pallas_call | solution.py:402
  178.4 1.0 copy.13
Async XLA Ops:
  0.0 56.7 %copy-start.6 = (s32[4]{0:T(128)S(1)}, s32[4]{0:T(128)}, u32[]{:S(2)}) copy-start(s32[4]{0:T(128)} %len_ref.3) | copy-start | bytes 52
  56.7 1.5 copy-start.1
  58.2 1.5 copy-start.2
  59.7 1.2 copy-start.4
  60.9 61.5 %copy-start.5 = (bf16[224,1280]{1,0:T(8,128)(2,1)S(1)}, bf16[224,1280]{1,0:T(8,128)(2,1)}, u32[]{:S(2)}) copy-start(bf16[224,1280]{1,0:T(8,128)(2,1)} %get-tuple-element.12.hbuf) | copy-start | bytes 1720324
  121.0 1.5 copy-start
  121.0 1.5 copy-start.7
  122.4 1.3 copy-start.3

commit v2 on v1

--- a/solution.py
+++ b/solution.py
@@ -11,7 +11,8 @@
 MESH = pl.DeviceIdType.MESH
 HS = 128
 GUIDE = 5.0
-BK = 512
+BK = 1536
+PAIR = 2
 ANY = pl.BlockSpec(memory_space=pl.ANY)
 SMEM = pl.BlockSpec(memory_space=pltpu.SMEM)
 
@@ -26,6 +27,10 @@
     active = jnp.logical_and(p % 3 < 2, p < 15)
     head = (p // 3) * 2 + p % 3
     return active, head, (s // 4) % 2
+
+
+def signal(semaphore, *device):
+    pl.semaphore_signal(semaphore, inc=1, device_id=device, device_id_type=MESH)
 
 
 def scatter_kernel(
@@ -38,6 +43,25 @@
     rows = q_ref.shape[1]
     heads = q_ref.shape[2] // HS
     half = hbuf.shape[1]
+    active, _, branch = role(s)
+    seqs = 32
+
+    barrier = pltpu.get_barrier_semaphore()
+    signal(barrier, 1 - b, s, g)
+
+    @pl.when(active)
+    def _():
+        @pl.loop(0, seqs)
+        def _(i):
+            t = (s + i) % seqs
+
+            @pl.when(jnp.logical_not(jnp.logical_and(t == s, branch == b)))
+            def _():
+                signal(barrier, branch, t, g)
+
+    own = jnp.where(jnp.logical_and(active, branch == b), 1, 0)
+    pl.semaphore_wait(barrier, 2 * heads + 1 - own)
+
     groups = kv_sem.shape[0]
     per = kbuf.shape[0] // groups
 
@@ -92,8 +116,6 @@
 
     other.start()
 
-    active, _, _ = role(s)
-
     def forward(buf, n):
         part = buf.at[pl.ds(n * per, per), :]
         return pltpu.make_async_remote_copy(
@@ -123,15 +145,16 @@
     other.wait()
 
 
-def attention_kernel(len_ref, q_ref, k_ref, v_ref, o_ref, s_ref, m_ref, l_ref, acc_ref):
+def attention_kernel(len_ref, q_ref, k_ref, v_ref, o_ref, s_ref, m_ref, acc_ref):
     c = lax.axis_index("cfg")
     s = lax.axis_index("seq")
     active, _, _ = role(s)
     rows = q_ref.shape[0]
+    piece = rows // PAIR
     tokens = k_ref.shape[0]
     factor = math.log2(math.e) / math.sqrt(HS)
-    first = (2 * pl.program_id(0) + c) * rows
-    last = first + rows - 1
+    first = (2 * PAIR * pl.program_id(0) + c) * piece
+    last = first + (2 * PAIR - 1) * piece - 1
     e0 = len_ref[0]
     e1 = e0 + len_ref[1]
     e2 = e1 + len_ref[2]
@@ -157,57 +180,68 @@
         base = (lo // 32) * 32
         blocks = pl.cdiv(hi - base, BK)
         single = seg_first == seg_last
-        seg_q = segment(first + lax.broadcasted_iota(jnp.int32, (rows, 1), 0))
-        q = q_ref[...]
+        row = lax.broadcasted_iota(jnp.int32, (rows, 1), 0)
+        seg_q = segment(first + row + (row // piece) * piece)
         m_ref[...] = jnp.full_like(m_ref, -1e30)
 
-        def lanes(x, op):
-            out = x[:, :HS]
-            for n in range(1, BK // HS):
-                out = op(out, x[:, n * HS : (n + 1) * HS])
-            return out
+        def widest(x):
+            out = m_ref[...]
+            for n in range(BK // HS):
+                out = jnp.maximum(out, x[:, n * HS : (n + 1) * HS])
+            m_ref[...] = out
+
+        def scores(at):
+            return lax.dot_general(
+                q_ref[...], k_ref[pl.ds(at, BK), :], (((1,), (1,)), ((), ())),
+                preferred_element_type=jnp.float32,
+            )
 
         @pl.loop(0, blocks)
         def _(n):
             logical = base + n * BK
             at = pl.multiple_of(jnp.minimum(logical, tokens - BK), 32)
-            score = lax.dot_general(
-                q, k_ref[pl.ds(at, BK), :], (((1,), (1,)), ((), ())),
-                preferred_element_type=jnp.float32,
-            )
             whole = jnp.logical_and(
                 single, jnp.logical_and(logical >= lo, logical + BK <= hi)
             )
 
             @pl.when(whole)
             def _():
+                score = scores(at)
                 s_ref[n] = score
-                m_ref[...] = jnp.maximum(m_ref[...], lanes(score, jnp.maximum))
+                widest(score)
 
             @pl.when(jnp.logical_not(whole))
             def _():
                 pos = at + lax.broadcasted_iota(jnp.int32, (1, BK), 1)
                 seg_k = jnp.where(pos >= logical, segment(pos), -1)
-                masked = jnp.where(seg_q == seg_k, score, -jnp.inf)
-                s_ref[n] = masked
-                m_ref[...] = jnp.maximum(m_ref[...], lanes(masked, jnp.maximum))
-
-        top = jnp.max(m_ref[...], axis=1, keepdims=True)
-        l_ref[...] = jnp.zeros_like(l_ref)
+                score = jnp.where(seg_q == seg_k, scores(at), -jnp.inf)
+                s_ref[n] = score
+                widest(score)
+
+        m_ref[...] = jnp.broadcast_to(
+            jnp.max(m_ref[...], axis=1, keepdims=True), m_ref.shape
+        )
         acc_ref[...] = jnp.zeros_like(acc_ref)
 
         @pl.loop(0, blocks)
         def _(n):
             at = pl.multiple_of(jnp.minimum(base + n * BK, tokens - BK), 32)
-            weight = jnp.exp2((s_ref[n] - top) * factor)
-            l_ref[...] += lanes(weight, jnp.add)
-            acc_ref[...] += jnp.dot(
-                weight.astype(jnp.bfloat16), v_ref[pl.ds(at, BK), :],
-                preferred_element_type=jnp.float32,
+            top = m_ref[...]
+            weight = jnp.concatenate(
+                [
+                    jnp.exp2((s_ref[n, :, j * HS : (j + 1) * HS] - top) * factor).astype(
+                        jnp.bfloat16
+                    )
+                    for j in range(BK // HS)
+                ],
+                axis=1,
             )
-
-        total = jnp.sum(l_ref[...], axis=1, keepdims=True)
-        o_ref[...] = (acc_ref[...] / total).astype(o_ref.dtype)
+            values = jnp.concatenate(
+                [v_ref[pl.ds(at, BK), :], jnp.ones((BK, HS), jnp.bfloat16)], axis=1
+            )
+            acc_ref[...] += jnp.dot(weight, values, preferred_element_type=jnp.float32)
+
+        o_ref[...] = (acc_ref[:, :HS] / acc_ref[:, HS:]).astype(o_ref.dtype)
 
 
 def project_kernel(
@@ -223,6 +257,21 @@
     width = 2 * half
     blocks = o_ref.shape[0] // rows
     mine = pl.multiple_of(b * half, half)
+
+    barrier = pltpu.get_barrier_semaphore()
+    signal(barrier, 1 - b, s, g)
+    signal(barrier, b, s, 1 - g)
+
+    @pl.loop(0, half // HS)
+    def _(i):
+        t = place((i + s) % (half // HS), b)
+
+        @pl.when(jnp.logical_not(jnp.logical_and(t == s, s % 2 == b)))
+        def _():
+            signal(barrier, s % 2, t, g)
+
+    own = jnp.where(jnp.logical_and(branch == b, s % 2 == b), 1, 0)
+    pl.semaphore_wait(barrier, 2 + jnp.where(active, blocks - own, 0))
 
     loads = [
         (down_ref, downv),
@@ -371,27 +420,27 @@
         in_specs=[ANY] * 4,
         out_specs=(ANY,) * 4,
         scratch_shapes=[dma((30,)), dma((4,)), dma, dma((2,)), dma((2, 4))],
-        compiler_params=pltpu.CompilerParams(has_side_effects=True),
+        compiler_params=pltpu.CompilerParams(has_side_effects=True, collective_id=1),
         name="scatter_heads",
     )(queries, keys, values, hidden)
 
     steps = tokens // 2 // rows
+    tile = PAIR * rows
     o = pl.pallas_call(
         attention_kernel,
-        grid=(steps,),
+        grid=(steps // PAIR,),
         out_shape=jax.ShapeDtypeStruct((tokens // 2, HS), bf16),
         in_specs=[
             SMEM,
-            pl.BlockSpec((rows, HS), lambda i: (i, 0)),
+            pl.BlockSpec((tile, HS), lambda i: (i, 0)),
             pl.BlockSpec((tokens, HS), lambda i: (0, 0)),
             pl.BlockSpec((tokens, HS), lambda i: (0, 0)),
         ],
-        out_specs=pl.BlockSpec((rows, HS), lambda i: (i, 0)),
+        out_specs=pl.BlockSpec((tile, HS), lambda i: (i, 0)),
         scratch_shapes=[
-            pltpu.VMEM((tokens // BK + 1, rows, BK), f32),
-            pltpu.VMEM((rows, HS), f32),
-            pltpu.VMEM((rows, HS), f32),
-            pltpu.VMEM((rows, HS), f32),
+            pltpu.VMEM((pl.cdiv(tokens, BK), tile, BK), f32),
+            pltpu.VMEM((tile, HS), f32),
+            pltpu.VMEM((tile, 2 * HS), f32),
         ],
         compiler_params=pltpu.CompilerParams(vmem_limit_bytes=48 * 2**20),
         name="attend",
@@ -422,7 +471,7 @@
             dma((6,)), dma((steps,)), dma, dma((2,)), dma((half // cols, 2)), dma((2,)), dma((3,)),
         ],
         compiler_params=pltpu.CompilerParams(
-            has_side_effects=True, vmem_limit_bytes=48 * 2**20
+            has_side_effects=True, collective_id=2, vmem_limit_bytes=48 * 2**20
         ),
         name="project",
     )(request_length, request_adapters, o, hidden, hbuf, output_weight, down, up)

time: 180 us -> 124 us (0.69)
  Pallas kernels: 171 us -> 115 us
    pallas_call x1, Pallas kernels: 60.1 us -> 24.6 us  [local(): pl.pallas_call(attention_kernel, grid=(steps // PAIR,), out_shape=jax.Sha...]
    pallas_call x1, Pallas kernels: 54.6 us -> 39.7 us  [local(): pl.pallas_call(project_kernel, out_shape=jax.ShapeDtypeStruct((rows, 2 *...]
    pallas_call x1, Pallas kernels: 56.7 us -> 50.4 us  [local(): pl.pallas_call(scatter_kernel, out_shape=(jax.ShapeDtypeStruct((tokens, H...]
where the time goes in v2:
time: 124 us; the launch traced here: 123 us
  Pallas kernels  115 us (93%)
  local copies, waits for them, and re-layouts  7.92 us (6%)
    pallas_call x1, Pallas kernels, local(): pl.pallas_call(scatter_kernel, out_shape=(jax.ShapeDtypeStruct((tokens, H...  50.4 us
    pallas_call x1, Pallas kernels, local(): pl.pallas_call(project_kernel, out_shape=jax.ShapeDtypeStruct((rows, 2 *...  39.7 us
    pallas_call x1, Pallas kernels, local(): pl.pallas_call(attention_kernel, grid=(steps // PAIR,), out_shape=jax.Sha...  24.6 us
    unnamed x17, local copies, waits for them, and re-layouts  6.51 us

profile of v2, /device:TPU:1, one launch (start us, length us, event | category | flops | bytes accessed | tf_op | source)
XLA Modules:
  0.0 122.8 jit_solution(336395849309044771)
XLA Ops:
  0.0 0.0 copy-start.6
  0.0 50.4 %scatter_heads.1 = (bf16[7168,128]{1,0:T(8,128)(2,1)}, bf16[7168,128]{1,0:T(8,128)(2,1)}, bf16[3584,128]{1,0:T(8,128)(2,1)}, bf16[224,1280]{1,0:T(8,128)(2,1)}) custom-call(bf16[1,224,1280]{2,1,0:T(8,128)(2,1)} %q_ref.1, bf16[1,224,1280]{2,1,0:T(8,128)(2,1)} %k_ref.1, bf16[1,224,1280]{2,1,0:T(8,128)(2,1)} %v_ref.1, bf16[1,224,2560]{2,1,0:T(8,128)(2,1)} %hid_ref.3), custom_call_target="tpu_custom_call" | custom-call | tf_op jit(solution)/shard_map/scatter_heads/pallas_call | solution.py:412
  50.5 0.0 copy-done.6
  50.5 0.0 copy-start.1
  50.5 1.5 %copy-done.1 = bf16[7168,128]{1,0:T(8,128)(2,1)S(1)} copy-done((bf16[7168,128]{1,0:T(8,128)(2,1)S(1)}, bf16[7168,128]{1,0:T(8,128)(2,1)}, u32[]{:S(2)}) %copy-start.1) | copy-done | bytes 1835032
  52.0 0.0 copy-start.2
  52.0 1.5 %copy-done.2 = bf16[7168,128]{1,0:T(8,128)(2,1)S(1)} copy-done((bf16[7168,128]{1,0:T(8,128)(2,1)S(1)}, bf16[7168,128]{1,0:T(8,128)(2,1)}, u32[]{:S(2)}) %copy-start.2) | copy-done | bytes 1835032
  53.5 0.0 copy-start.4
  53.5 1.2 copy-done.4
  54.6 0.0 copy-start.5
  54.7 24.6 %attend.1.o_ref = bf16[3584,128]{1,0:T(8,128)(2,1)S(1)} custom-call(s32[4]{0:T(128)S(1)} %copy-done.6, bf16[3584,128]{1,0:T(8,128)(2,1)S(1)} %copy-done.4, bf16[7168,128]{1,0:T(8,128)(2,1)S(1)} %copy-done.1, bf16[7168,128]{1,0:T(8,128)(2,1)S(1)} %copy-done.2), custom_call_target="tpu_custom_call" | custom-call | tf_op jit(solution)/shard_map/attend/pallas_call | solution.py:429
  79.2 0.0 copy-start
  79.2 0.0 copy-start.7
  79.2 1.4 %copy.11.down_ref = bf16[1280,256]{1,0:T(8,128)(2,1)S(1)} copy(bf16[1280,256]{0,1:T(8,128)(2,1)} %bitcast.5) | data formatting | bytes 1310720 | tf_op jit(solution)/shard_map/reshape | solution.py:408
  80.7 0.0 copy-done.5
  80.7 0.0 copy-done
  80.7 0.0 copy-done.7
  80.7 0.0 copy-start.3
  80.7 1.3 %copy-done.3 = bf16[8,32,2560]{2,1,0:T(8,128)(2,1)S(1)} copy-done((bf16[8,32,2560]{2,1,0:T(8,128)(2,1)S(1)}, bf16[8,32,2560]{2,1,0:T(8,128)(2,1)}, u32[]{:S(2)}) %copy-start.3) | copy-done | bytes 1310744
  82.0 39.7 %project.1 = bf16[224,2560]{1,0:T(8,128)(2,1)S(1)} custom-call(s32[4]{0:T(128)S(1)} %copy-done.6, s32[4]{0:T(128)S(1)} %copy-done.7, bf16[3584,128]{1,0:T(8,128)(2,1)S(1)} %attend.1.o_ref, bf16[1,224,2560]{2,1,0:T(8,128)(2,1)S(1)} %copy-done, bf16[224,1280]{1,0:T(8,128)(2,1)S(1)} %copy-done.5, bf16[1280,5120]{1,0:T(8,128)(2,1)} %w_ref.1, ...), custom_call_target="tpu_custom_call" | custom-call | tf_op jit(solution)/shard_map/project/pallas_call | solution.py:451
  121.8 1.0 copy.13
Async XLA Ops:
  0.0 50.5 %copy-start.6 = (s32[4]{0:T(128)S(1)}, s32[4]{0:T(128)}, u32[]{:S(2)}) copy-start(s32[4]{0:T(128)} %len_ref.3) | copy-start | bytes 52
  50.5 1.5 %copy-start.1 = (bf16[7168,128]{1,0:T(8,128)(2,1)S(1)}, bf16[7168,128]{1,0:T(8,128)(2,1)}, u32[]{:S(2)}) copy-start(bf16[7168,128]{1,0:T(8,128)(2,1)} %get-tuple-element.10.k_ref) | copy-start | bytes 5505028
  52.0 1.5 %copy-start.2 = (bf16[7168,128]{1,0:T(8,128)(2,1)S(1)}, bf16[7168,128]{1,0:T(8,128)(2,1)}, u32[]{:S(2)}) copy-start(bf16[7168,128]{1,0:T(8,128)(2,1)} %get-tuple-element.11.v_ref) | copy-start | bytes 5505028
  53.5 1.2 copy-start.4
  54.6 26.0 %copy-start.5 = (bf16[224,1280]{1,0:T(8,128)(2,1)S(1)}, bf16[224,1280]{1,0:T(8,128)(2,1)}, u32[]{:S(2)}) copy-start(bf16[224,1280]{1,0:T(8,128)(2,1)} %get-tuple-element.12.hbuf) | copy-start | bytes 1720324
  79.2 1.5 %copy-start = (bf16[1,224,2560]{2,1,0:T(8,128)(2,1)S(1)}, bf16[1,224,2560]{2,1,0:T(8,128)(2,1)}, u32[]{:S(2)}) copy-start(bf16[1,224,2560]{2,1,0:T(8,128)(2,1)} %hid_ref.3) | copy-start | bytes 3440644
  79.2 1.5 %copy-start.7 = (s32[4]{0:T(128)S(1)}, s32[4]{0:T(128)}, u32[]{:S(2)}) copy-start(s32[4]{0:T(128)} %ad_ref.1) | copy-start | bytes 52
  80.7 1.3 %copy-start.3 = (bf16[8,32,2560]{2,1,0:T(8,128)(2,1)S(1)}, bf16[8,32,2560]{2,1,0:T(8,128)(2,1)}, u32[]{:S(2)}) copy-start(bf16[8,32,2560]{2,1,0:T(8,128)(2,1)} %param.15) | copy-start | bytes 3932164
